TPU v7x, 512 devices: a whole 4x8x8 slice. The times are simulated.
512 devices in a mesh: outer: 8 (over x, y_hi), rep: 4 (over y_lo), shard: 16 (over z, core).
Axes of the slice: x: 4, y: 8 (y_hi: 2, y_lo: 4; y = y_hi * 4 + y_lo), z: 8, core: 2. Of those that a mesh axis runs over, the one named last changes fastest.
Arguments:
- momentum: float32 [8, 4, 1024, 8192], P('outer', 'rep', 'shard'), may hold values from -6 to 6
Outputs:
- new_momentum: float32 [8, 4, 1024, 8192], P('outer', 'rep', 'shard')
- update: bfloat16 [8, 1024, 8192], P('outer', 'shard')
All inputs are finite; a program needn't handle non-finite values.
Results may differ from a plain program's by a relative error of at most 0.001.
Values sent between devices are 32-bit elements; how exact they have to be, the bound alone decides.
A program may use at most 64 MiB of HBM per device.

v0:
```python
import jax
import jax.numpy as jnp
from jax import lax
from jax.sharding import PartitionSpec as P

TILE = 64
KEEP = 16


def from_behind(block, axis, distance):
    devices = range(lax.axis_size(axis))
    route = [((i - distance) % len(devices), i) for i in devices]
    return lax.ppermute(block, axis, route)


def low_basis():
    index = jnp.arange(TILE).astype(jnp.float32)
    freq = jnp.arange(KEEP).astype(jnp.float32)
    angles = jnp.pi * (2.0 * index[None, :] + 1.0) * freq[:, None] / (2.0 * TILE)
    scales = jnp.where(freq == 0.0, jnp.sqrt(1.0 / TILE), jnp.sqrt(2.0 / TILE)).astype(jnp.float32)
    return scales[:, None] * jnp.cos(angles)


def encode(block, basis):
    rows, cols = block.shape
    tiled = block.reshape(rows // TILE, TILE, cols)
    left = jnp.einsum("kr,trd->tkd", basis, tiled, precision=lax.Precision.HIGHEST)
    left = left.reshape(rows // TILE, KEEP, cols // TILE, TILE)
    return jnp.einsum("tknc,lc->tknl", left, basis, precision=lax.Precision.HIGHEST)


def decode(coeffs, basis):
    tiles, keep, ncol, keep2 = coeffs.shape
    right = jnp.einsum("tknl,lc->tknc", coeffs, basis, precision=lax.Precision.HIGHEST)
    right = right.reshape(tiles, KEEP, ncol * TILE)
    full = jnp.einsum("kr,tkd->trd", basis, right, precision=lax.Precision.HIGHEST)
    return full.reshape(tiles * TILE, ncol * TILE)


def neighbours(values):
    below = from_behind(values, "outer", 1)
    above = from_behind(values, "outer", -1)
    return 0.5 * values + 0.25 * (below + above)


def local(momentum):
    block = momentum[0, 0]
    basis = low_basis()
    coeffs = encode(block, basis)
    tiles, keep, ncol, keep2 = coeffs.shape
    flat = coeffs.reshape(tiles, keep, ncol * keep2)
    pod_total = lax.psum(flat, "rep")
    mixed = neighbours(pod_total)
    update = decode(mixed.reshape(tiles, keep, ncol, keep2), basis).astype(jnp.bfloat16)
    fresh = block - decode(coeffs, basis)
    return (fresh[None, None], update[None])


def solution(mesh):
    in_specs = (P("outer", "rep", "shard", None),)
    out_specs = (P("outer", "rep", "shard", None), P("outer", "shard", None))
    return jax.shard_map(local, mesh=mesh, in_specs=in_specs, out_specs=out_specs, check_vma=False)
```

profile of v0, /device:TPU:24, one launch (start us, length us, event | category | flops | bytes accessed | tf_op | source)
XLA Modules:
  0.0 105.0 jit_solution(16406080387587127392)
XLA Ops:
  7.2 0.0 all-reduce.2.cloned.1.call-start
  7.2 2.8 %convolution_bitcast_fusion.1 = f32[1,16,8192]{2,1,0:T(8,128)S(1)} fusion(f32[1,1,64,8192]{3,2,1,0:T(8,128)} %param.1, f32[16]{0:T(128)S(1)} %iota_convert_fusion, f32[64]{0:T(128)S(1)} %add_multiply_fusion, f32[16]{0:T(128)S(1)} %compare_select_fusion), kind=kOutput, calls=%fused_computation.4 | convolution fusion | flops 100666368 | bytes 2621824 | tf_op jit(solution)/shard_map/kr,trd->tkd/dot_general | solution.py:27
  10.0 0.4 reshape.67
  10.4 1.1 %fusion.7 = f32[16,128,16]{1,2,0:T(8,128)S(1)} fusion(f32[16,128,64]{2,1,0:T(8,128)S(1)} %reshape.67, f32[16]{0:T(128)S(1)} %iota_convert_fusion, f32[64]{0:T(128)S(1)} %add_multiply_fusion, f32[16]{0:T(128)S(1)} %compare_select_fusion), kind=kOutput, calls=%fused_computation.11 | convolution fusion | flops 25168896 | bytes 655744 | tf_op jit(solution)/shard_map/tknc,lc->tknl/dot_general | solution.py:29
  11.5 0.3 copy.6
  11.8 0.0 copy-start
  11.8 1.3 %reshape.70 = f32[1,16,2048]{2,1,0:T(8,128)} reshape(f32[16,128,16]{2,1,0:T(8,128)S(1)} %copy.6) | data formatting | bytes 262144 | tf_op jit(solution)/shard_map/reshape | solution.py:51
  13.1 0.0 all-reduce.2.cloned.1.call-update
  13.2 1.8 %fusion.5 = f32[16,128,64]{2,1,0:T(8,128)S(1)} fusion(f32[16,128,16]{1,2,0:T(8,128)S(1)} %fusion.7, f32[16]{0:T(128)S(1)} %iota_convert_fusion, f32[64]{0:T(128)S(1)} %add_multiply_fusion, f32[16]{0:T(128)S(1)} %compare_select_fusion), kind=kOutput, calls=%fused_computation.9 | convolution fusion | flops 25168896 | bytes 655744 | tf_op jit(solution)/shard_map/tknl,lc->tknc/dot_general | solution.py:34
  15.0 1.2 %reshape.68 = f32[16,8192]{1,0:T(8,128)} reshape(f32[16,128,64]{2,1,0:T(8,128)S(1)} %fusion.5) | data formatting | bytes 1048576 | tf_op jit(solution)/shard_map/reshape.14
  16.1 53.6 %all-reduce.2.cloned.1.call-done = f32[1,16,2048]{2,1,0:T(8,128)} async-done(((f32[1,16,2048]{2,1,0:T(8,128)}), f32[1,16,2048]{2,1,0:T(8,128)}) %all-reduce.2.cloned.1.call-update) | async-done | bytes 131088 | tf_op jit(solution)/shard_map/psum | solution.py:52
  69.7 0.0 copy-start.1
  69.7 8.6 %collective-permute-start.1 = (f32[1,16,2048]{2,1,0:T(8,128)}, f32[1,16,2048]{2,1,0:T(8,128)S(1)}, u32[]{:S(2)}, u32[]{:S(2)}) collective-permute-start(f32[1,16,2048]{2,1,0:T(8,128)} %all-reduce.2.cloned.1.call-done), channel_id=1, source_target_pairs={{64,0},{128,64},{192,128},{256,192},{320,256},{384,320},{448,384},... | collective-permute-start | bytes 393224 | tf_op jit(solution)/shard_map/ppermute | solution.py:13
  78.3 1.9 %collective-permute-start = (f32[1,16,2048]{2,1,0:T(8,128)}, f32[1,16,2048]{2,1,0:T(8,128)S(1)}, u32[]{:S(2)}, u32[]{:S(2)}) collective-permute-start(f32[1,16,2048]{2,1,0:T(8,128)} %all-reduce.2.cloned.1.call-done), channel_id=1, source_target_pairs={{448,0},{0,64},{64,128},{128,192},{192,256},{256,320},{320,384},{3... | collective-permute-start | bytes 393224 | tf_op jit(solution)/shard_map/ppermute | solution.py:13
  80.3 0.0 copy-done
  80.3 4.3 %fusion = f32[1,1,64,8192]{3,2,1,0:T(8,128)} fusion(f32[1,1,64,8192]{3,2,1,0:T(8,128)S(1)} %copy-done, f32[16,8192]{1,0:T(8,128)} %reshape.68, f32[16]{0:T(128)S(1)} %iota_convert_fusion, f32[64]{0:T(128)S(1)} %add_multiply_fusion, f32[16]{0:T(128)S(1)} %compare_select_fusion), kind=kOutput, calls=%fused_computation.1 | convolution fusion | flops 101190656 | bytes 4718976 | tf_op jit(solution)/shard_map/kr,tkd->trd/dot_general | solution.py:36
  84.6 0.0 collective-permute-done.1
  84.6 8.8 %collective-permute-done = f32[1,16,2048]{2,1,0:T(8,128)S(1)} collective-permute-done((f32[1,16,2048]{2,1,0:T(8,128)}, f32[1,16,2048]{2,1,0:T(8,128)S(1)}, u32[]{:S(2)}, u32[]{:S(2)}) %collective-permute-start) | collective-permute-done | bytes 131104 | tf_op jit(solution)/shard_map/ppermute | solution.py:13
  93.4 0.0 copy-done.1
  93.5 0.4 reshape.71
  93.8 1.1 %fusion.3 = f32[16,128,64]{2,1,0:T(8,128)S(1)} fusion(f32[16,128,16]{2,1,0:T(8,128)S(1)} %reshape.71, f32[16]{0:T(128)S(1)} %iota_convert_fusion, f32[64]{0:T(128)S(1)} %add_multiply_fusion, f32[16]{0:T(128)S(1)} %compare_select_fusion), kind=kOutput, calls=%fused_computation.7 | convolution fusion | flops 25168896 | bytes 655744 | tf_op jit(solution)/shard_map/tknl,lc->tknc/dot_general | solution.py:34
  94.9 0.4 reshape.72
  95.3 2.9 %fusion.1 = bf16[1,64,8192]{2,1,0:T(8,128)(2,1)} fusion(f32[16,8192]{1,0:T(8,128)S(1)} %reshape.72, f32[16]{0:T(128)S(1)} %iota_convert_fusion, f32[64]{0:T(128)S(1)} %add_multiply_fusion, f32[16]{0:T(128)S(1)} %compare_select_fusion), kind=kOutput, calls=%fused_computation.3 | convolution fusion | flops 101190656 | bytes 1573248 | tf_op jit(solution)/shard_map/kr,tkd->trd/dot_general | solution.py:36
  (4 shorter events, 0.0 us)
Async XLA Ops:
  7.2 62.5 %all-reduce.2.cloned.1.call-start = ((), (), s32[]{:S(2)}) async-start(), calls=%async_computation | async-start | bytes 262144 | tf_op jit(solution)/shard_map/psum | solution.py:52
  11.8 68.4 %copy-start = (f32[1,1,64,8192]{3,2,1,0:T(8,128)S(1)}, f32[1,1,64,8192]{3,2,1,0:T(8,128)}, u32[]{:S(2)}) copy-start(f32[1,1,64,8192]{3,2,1,0:T(8,128)} %param.1) | copy-start | bytes 6291460
  69.7 23.7 %copy-start.1 = (f32[1,16,2048]{2,1,0:T(8,128)S(1)}, f32[1,16,2048]{2,1,0:T(8,128)}, u32[]{:S(2)}) copy-start(f32[1,16,2048]{2,1,0:T(8,128)} %all-reduce.2.cloned.1.call-done) | copy-start | bytes 393220
  69.7 14.9 %collective-permute-start.1 = (f32[1,16,2048]{2,1,0:T(8,128)}, f32[1,16,2048]{2,1,0:T(8,128)S(1)}, u32[]{:S(2)}, u32[]{:S(2)}) collective-permute-start(f32[1,16,2048]{2,1,0:T(8,128)} %all-reduce.2.cloned.1.call-done), channel_id=1, source_target_pairs={{64,0},{128,64},{192,128},{256,192},{320,256},{384,320},{448,384},... | collective-permute-start | bytes 393224 | tf_op jit(solution)/shard_map/ppermute | solution.py:13
  78.3 15.1 %collective-permute-start = (f32[1,16,2048]{2,1,0:T(8,128)}, f32[1,16,2048]{2,1,0:T(8,128)S(1)}, u32[]{:S(2)}, u32[]{:S(2)}) collective-permute-start(f32[1,16,2048]{2,1,0:T(8,128)} %all-reduce.2.cloned.1.call-done), channel_id=1, source_target_pairs={{448,0},{0,64},{64,128},{128,192},{192,256},{256,320},{320,384},{3... | collective-permute-start | bytes 393224 | tf_op jit(solution)/shard_map/ppermute | solution.py:13
Sparse Core Ops, SparseCore 0:
  13.3 56.3 all-reduce.1
where the time goes:
time: 105 us
  waiting for transfers between devices  62.4 us (59%)
  between operations  14.1 us (13%)
  matrix products  14 us (13%)
  starting transfers between devices  10.6 us (10%)
  local copies, waits for them, and re-layouts  3.91 us (4%)
    psum x1, waiting for transfers between devices, local(): pod_total = lax.psum(flat, 'rep')  53.6 us
    ppermute x2, starting transfers between devices, from_behind(): return lax.ppermute(block, axis, route)  10.5 us
    ppermute x2, waiting for transfers between devices, from_behind(): return lax.ppermute(block, axis, route)  8.83 us
    dot_general x2, matrix products, decode(): jnp.einsum('kr,tkd->trd', basis, right, precision=lax.Precision.HIGHEST)  7.24 us
    dot_general x2, matrix products, decode(): jnp.einsum('tknl,lc->tknc', coeffs, basis, precision=lax.Precision.HIGHEST)  2.91 us
    dot_general x1, matrix products, encode(): jnp.einsum('kr,trd->tkd', basis, tiled, precision=lax.Precision.HIGHEST)  2.76 us
    another operation x4, local copies, waits for them, and re-layouts  2.28 us
  transfers between devices with their start and end apart: 3, of which 2 were waited for; matrix products, arithmetic and copies ran while one was open for 7% of the time, Pallas kernels for 0%

commit v1 on v0

v1 whole, which is shorter than its diff:
```python
import functools

import jax
import jax.numpy as jnp
import ml_dtypes
import numpy as np
from jax import lax
from jax.experimental import pallas as pl
from jax.experimental.pallas import tpu as pltpu
from jax.sharding import PartitionSpec as P

TILE = 64
KEEP = 16
RING = 8
POD = 4
GROUP = 8
MESH = pl.DeviceIdType.MESH
BF16 = jnp.bfloat16
F32 = jnp.float32


def low_basis():
    index = np.arange(TILE)
    freq = np.arange(KEEP)
    angles = np.pi * (2.0 * index[None, :] + 1.0) * freq[:, None] / (2.0 * TILE)
    scales = np.where(freq == 0, np.sqrt(1.0 / TILE), np.sqrt(2.0 / TILE))
    return (scales[:, None] * np.cos(angles)).astype(np.float32)


def halves(array):
    high = array.astype(ml_dtypes.bfloat16)
    low = (array - high.astype(np.float32)).astype(ml_dtypes.bfloat16)
    return high, low


def tables():
    basis = low_basis()
    high, low = (half.astype(np.float32) for half in halves(basis))
    out = np.zeros((208, 256), np.float32)
    out[:128, :128] = np.tile(basis, (GROUP, 2))
    out[:128, 128:] = np.tile(basis.T, (2, GROUP))
    out[128:144, :192] = np.concatenate([high, low, high], axis=1)
    out[144:, :48] = np.concatenate([high.T, high.T, low.T], axis=1)
    return out


def set_up(table, enc_cols, enc_rows, dec_cols, dec_rows):
    for place in range(4):
        lanes = pl.ds(place * 128, 128)
        row = lax.broadcasted_iota(jnp.int32, (128, 128), 0)
        col = lax.broadcasted_iota(jnp.int32, (128, 128), 1)
        high, low = split(jnp.where(row // KEEP == 2 * place + col // TILE, table[:128, :128], 0.0))
        dec_cols[:128, lanes] = high
        dec_cols[128:256, lanes] = high
        dec_cols[256:, lanes] = low
        high, low = split(jnp.where(col // KEEP == 2 * place + row // TILE, table[:128, 128:], 0.0))
        enc_cols[lanes, :128] = high
        enc_cols[lanes, 128:] = low
    enc_rows[...] = table[128:144, :192].astype(BF16)
    dec_rows[...] = table[144:, :48].astype(BF16)


def split(value):
    high = value.astype(BF16)
    low = (value - high.astype(F32)).astype(BF16)
    return high, low


def dot(a, b):
    return jnp.dot(a, b, preferred_element_type=F32)


def encode(x, enc_cols, enc_rows):
    groups = x.shape[1] // (GROUP * TILE)
    tall = jnp.concatenate([x[:, g * 512:(g + 1) * 512] for g in range(groups)], axis=0)
    high, low = split(tall)
    both = dot(high, enc_cols[...])
    right = both[:, :128] + both[:, 128:] + dot(low, enc_cols[:, :128])
    right = jnp.concatenate([right[g * TILE:(g + 1) * TILE] for g in range(groups)], axis=1)
    high, low = split(right)
    return dot(enc_rows[...], jnp.concatenate([high, high, low], axis=0))


def decode(c, dec_cols, dec_rows):
    groups = c.shape[1] // 128
    tall = jnp.concatenate([c[:, g * 128:(g + 1) * 128] for g in range(groups)], axis=0)
    high, low = split(tall)
    right = dot(jnp.concatenate([high, low, high], axis=1), dec_cols[...])
    right = jnp.concatenate([right[g * KEEP:(g + 1) * KEEP] for g in range(groups)], axis=1)
    high, low = split(right)
    return dot(dec_rows[...], jnp.concatenate([high, low, high], axis=0))


def kernel(x_hbm, table_hbm, fresh, update,
           x, table, enc_cols, enc_rows, dec_cols, dec_rows, coeffs, parts, sums, around, mixed, got,
           x_sem, table_sem, rs_send, rs_recv, x_send, x_recv, ag_send, ag_recv):
    outer, rep = lax.axis_index("outer"), lax.axis_index("rep")
    columns = lax.axis_size("outer") // 2
    column, side = outer // 2, outer % 2
    me = side * POD + rep
    width = x.shape[1] // RING
    kept = coeffs.shape[2]

    def ring(place):
        return {"outer": column * 2 + place // POD, "rep": place % POD}

    def beside(step):
        return {"outer": lax.rem(column + step + columns, columns) * 2 + side}

    def off(step):
        half = (step + 1) // 2
        return 4 + half * (1 - 2 * (step % 2))

    def chunk(place):
        return pl.ds(pl.multiple_of(place * width, width), width)

    def load(place):
        return pltpu.make_async_copy(x_hbm.at[0, 0, :, chunk(place)], x.at[:, chunk(place)], x_sem.at[place])

    def place_at(step):
        return lax.rem(me + off(step), RING)

    table_copy = pltpu.make_async_copy(table_hbm, table, table_sem)
    table_copy.start()
    for step in range(RING):
        load(place_at(step)).start()

    barrier = pltpu.get_barrier_semaphore()
    for step in range(1, RING):
        pl.semaphore_signal(barrier, inc=1, device_id=ring(lax.rem(me + step, RING)), device_id_type=MESH)
    for step in (1, -1):
        pl.semaphore_signal(barrier, inc=1, device_id=beside(step), device_id_type=MESH)

    def encode_at(place):
        load(place).wait()
        coeffs[place] = encode(x[:, chunk(place)], enc_cols, enc_rows)

    def share(place):
        return pltpu.make_async_remote_copy(
            src_ref=coeffs.at[place], dst_ref=parts.at[me], send_sem=rs_send.at[place], recv_sem=rs_recv.at[me],
            device_id=ring(place), device_id_type=MESH)

    def arrived(place):
        return pltpu.make_async_remote_copy(
            src_ref=coeffs.at[place], dst_ref=parts.at[place], send_sem=rs_send.at[place], recv_sem=rs_recv.at[place],
            device_id=ring(place), device_id_type=MESH)

    table_copy.wait()
    set_up(table, enc_cols, enc_rows, dec_cols, dec_rows)
    encode_at(place_at(0))
    pl.semaphore_wait(barrier, RING + 1)
    share(place_at(0)).start()

    @pl.loop(1, RING - 1)
    def _(step):
        place = place_at(step)
        encode_at(place)
        share(place).start()

    encode_at(me)
    parts[me] = coeffs[me]

    @pl.loop(0, RING)
    def _(place):
        fresh[0, 0, :, chunk(place)] = x[:, chunk(place)] - decode(coeffs[place], dec_cols, dec_rows)

    @pl.loop(1, RING)
    def _(step):
        arrived(lax.rem(me + step, RING)).wait_recv()

    sums[0] = parts[0] + parts[1] + parts[2] + parts[3]
    sums[1] = parts[4] + parts[5] + parts[6] + parts[7]
    to_next = pltpu.make_async_remote_copy(
        src_ref=sums.at[1], dst_ref=around.at[0], send_sem=x_send.at[0], recv_sem=x_recv.at[0],
        device_id=beside(1), device_id_type=MESH)
    to_prev = pltpu.make_async_remote_copy(
        src_ref=sums.at[0], dst_ref=around.at[1], send_sem=x_send.at[1], recv_sem=x_recv.at[1],
        device_id=beside(-1), device_id_type=MESH)
    to_next.start()
    to_prev.start()
    first = 0.5 * sums[0] + 0.25 * sums[1]
    second = 0.5 * sums[1] + 0.25 * sums[0]
    to_next.wait_recv()
    mixed[0] = first + 0.25 * around[0]
    to_prev.wait_recv()
    mixed[1] = second + 0.25 * around[1]

    def spread(place):
        return pltpu.make_async_remote_copy(
            src_ref=mixed.at[place // POD], dst_ref=got.at[me], send_sem=ag_send.at[place], recv_sem=ag_recv.at[me],
            device_id=ring(place), device_id_type=MESH)

    def landed(place):
        return pltpu.make_async_remote_copy(
            src_ref=mixed.at[0], dst_ref=got.at[place], send_sem=ag_send.at[place], recv_sem=ag_recv.at[place],
            device_id=ring(place), device_id_type=MESH)

    @pl.loop(0, RING - 1)
    def _(step):
        spread(place_at(step)).start()

    got[me] = mixed[side]

    def decode_at(place):
        update[0, :, chunk(place)] = decode(got[place], dec_cols, dec_rows).astype(BF16)

    decode_at(me)

    @pl.loop(1, RING)
    def _(step):
        place = place_at(RING - 1 - step)
        landed(place).wait_recv()
        decode_at(place)

    to_next.wait_send()
    to_prev.wait_send()

    @pl.loop(1, RING)
    def _(step):
        place = lax.rem(me + step, RING)
        share(place).wait_send()
        spread(place).wait_send()


def local(momentum):
    rows, cols = momentum.shape[2:]
    table = jnp.asarray(tables())
    kept = cols // TILE * KEEP // RING
    vmem = pl.BlockSpec(memory_space=pltpu.VMEM)
    block = (KEEP, kept)
    dma = pltpu.SemaphoreType.DMA
    return pl.pallas_call(
        kernel,
        out_shape=(
            pltpu.VMEM(momentum.shape, F32),
            pltpu.VMEM((1, rows, cols), BF16),
        ),
        in_specs=[pl.BlockSpec(memory_space=pltpu.HBM)] * 2,
        out_specs=(vmem, vmem),
        scratch_shapes=[
            pltpu.VMEM((rows, cols), F32),
            pltpu.VMEM(table.shape, F32),
            pltpu.VMEM((512, 256), BF16),
            pltpu.VMEM((16, 192), BF16),
            pltpu.VMEM((384, 512), BF16),
            pltpu.VMEM((64, 48), BF16),
            pltpu.VMEM((RING, *block), F32),
            pltpu.VMEM((RING, *block), F32),
            pltpu.VMEM((2, *block), F32),
            pltpu.VMEM((2, *block), F32),
            pltpu.VMEM((2, *block), F32),
            pltpu.VMEM((RING, *block), F32),
            dma((RING,)),
            dma,
            dma((RING,)),
            dma((RING,)),
            dma((2,)),
            dma((2,)),
            dma((RING,)),
            dma((RING,)),
        ],
        compiler_params=pltpu.CompilerParams(
            collective_id=0, has_side_effects=True, vmem_limit_bytes=60 * 1024 * 1024),
    )(momentum, table)


def solution(mesh):
    in_specs = (P("outer", "rep", "shard", None),)
    out_specs = (P("outer", "rep", "shard", None), P("outer", "shard", None))
    return jax.shard_map(local, mesh=mesh, in_specs=in_specs, out_specs=out_specs, check_vma=False)
```

time: 105 us -> 26.8 us (0.26)
  the two profiles are of different devices: /device:TPU:24 before, /device:TPU:384 now
where the time goes in v1:
time: 26.8 us; the launch traced here: 26.7 us
  Pallas kernels  23.8 us (89%)
  local copies, waits for them, and re-layouts  2.29 us (9%)
  between operations  0.64 us (2%)
    pallas_call x1, Pallas kernels, local(): pl.pallas_call(kernel, out_shape=(pltpu.VMEM(momentum.shape, F32), pltpu....  23.8 us
    unnamed x2, local copies, waits for them, and re-layouts  2.29 us

profile of v1, /device:TPU:384, one launch (start us, length us, event | category | flops | bytes accessed | tf_op | source)
XLA Modules:
  0.0 26.7 jit_solution(3514742302258921215)
XLA Ops:
  0.6 23.8 %shard_map.41 = (f32[1,1,64,8192]{3,2,1,0:T(8,128)S(1)}, bf16[1,64,8192]{2,1,0:T(8,128)(2,1)S(1)}) custom-call(f32[1,1,64,8192]{3,2,1,0:T(8,128)} %x_hbm.1, f32[208,256]{1,0:T(8,128)} %constant.2.clone.table_hbm), custom_call_target="tpu_custom_call" | custom-call | tf_op jit(solution)/shard_map/pallas_call | solution.py:232
  24.4 1.3 %copy.6 = f32[1,1,64,8192]{3,2,1,0:T(8,128)} copy(f32[1,1,64,8192]{3,2,1,0:T(8,128)S(1)} %get-tuple-element.2) | data formatting | bytes 4194304
  25.7 1.0 %copy.7 = bf16[1,64,8192]{2,1,0:T(8,128)(2,1)} copy(bf16[1,64,8192]{2,1,0:T(8,128)(2,1)S(1)} %get-tuple-element.3) | data formatting | bytes 2097152

commit v2 on v1

v2 whole, which is shorter than its diff:
```python
import functools

import jax
import jax.numpy as jnp
import ml_dtypes
import numpy as np
from jax import lax
from jax.experimental import pallas as pl
from jax.experimental.pallas import tpu as pltpu
from jax.sharding import PartitionSpec as P

TILE = 64
KEEP = 16
RING = 8
POD = 4
GROUP = 8
MESH = pl.DeviceIdType.MESH
BF16 = jnp.bfloat16
F32 = jnp.float32


def low_basis():
    index = np.arange(TILE)
    freq = np.arange(KEEP)
    angles = np.pi * (2.0 * index[None, :] + 1.0) * freq[:, None] / (2.0 * TILE)
    scales = np.where(freq == 0, np.sqrt(1.0 / TILE), np.sqrt(2.0 / TILE))
    return (scales[:, None] * np.cos(angles)).astype(np.float32)


def halves(array):
    high = array.astype(ml_dtypes.bfloat16)
    low = (array - high.astype(np.float32)).astype(ml_dtypes.bfloat16)
    return high, low


def tables():
    basis = low_basis()
    high, low = (half.astype(np.float32) for half in halves(basis))
    out = np.zeros((208, 256), np.float32)
    out[:128, :128] = np.tile(basis, (GROUP, 2))
    out[:128, 128:] = np.tile(basis.T, (2, GROUP))
    out[128:144, :192] = np.concatenate([high, low, high], axis=1)
    out[144:, :48] = np.concatenate([high.T, high.T, low.T], axis=1)
    return out


def set_up(table, enc_cols, enc_rows, dec_cols, dec_rows):
    for place in range(4):
        lanes = pl.ds(place * 128, 128)
        row = lax.broadcasted_iota(jnp.int32, (128, 128), 0)
        col = lax.broadcasted_iota(jnp.int32, (128, 128), 1)
        high, low = split(jnp.where(row // KEEP == 2 * place + col // TILE, table[:128, :128], 0.0))
        dec_cols[:128, lanes] = high
        dec_cols[128:256, lanes] = high
        dec_cols[256:, lanes] = low
        high, low = split(jnp.where(col // KEEP == 2 * place + row // TILE, table[:128, 128:], 0.0))
        enc_cols[lanes, :128] = high
        enc_cols[lanes, 128:] = low
    enc_rows[...] = table[128:144, :192].astype(BF16)
    dec_rows[...] = table[144:, :48].astype(BF16)


def split(value):
    high = value.astype(BF16)
    low = (value - high.astype(F32)).astype(BF16)
    return high, low


def dot(a, b):
    return jnp.dot(a, b, preferred_element_type=F32)


def encode(groups, enc_cols, enc_rows):
    high, low = split(jnp.concatenate(groups, axis=0))
    both = dot(high, enc_cols[...])
    right = both[:, :128] + both[:, 128:] + dot(low, enc_cols[:, :128])
    right = jnp.concatenate([right[g * TILE:(g + 1) * TILE] for g in range(len(groups))], axis=1)
    high, low = split(right)
    return dot(enc_rows[...], jnp.concatenate([high, high, low], axis=0))


def decode(blocks, dec_cols, dec_rows, put):
    high, low = split(jnp.concatenate(blocks, axis=0))
    right = dot(jnp.concatenate([high, low, high], axis=1), dec_cols[...])
    for g in range(len(blocks)):
        high, low = split(right[g * KEEP:(g + 1) * KEEP])
        put(g, dot(dec_rows[...], jnp.concatenate([high, low, high], axis=0)))


def kernel(x_hbm, table_hbm, fresh, update,
           x, table, enc_cols, enc_rows, dec_cols, dec_rows, coeffs, parts, sums, around, mixed, got,
           x_sem, table_sem, rs_send, rs_recv, swap_send, swap_recv, ag_send, ag_recv):
    outer, rep, shard = (lax.axis_index(axis) for axis in ("outer", "rep", "shard"))
    columns = lax.axis_size("outer") // 2
    column, side, core = outer // 2, outer % 2, shard % 2
    me = side * POD + rep
    wide = GROUP * TILE

    def ring(place, to_core):
        return {"outer": column * 2 + place // POD, "rep": place % POD, "shard": shard - core + to_core}

    def beside(step):
        return {"outer": lax.rem(column + step + columns, columns) * 2 + side}

    def place_at(step):
        half = (step + 1) // 2
        return lax.rem(me + 4 + half * (1 - 2 * (step % 2)), RING)

    def load(part):
        cols = pl.ds(part * 2 * wide, 2 * wide)
        return pltpu.make_async_copy(x_hbm.at[0, 0, :, cols], x.at[:, cols], x_sem.at[part])

    table_copy = pltpu.make_async_copy(table_hbm, table, table_sem)
    table_copy.start()
    for part in range(RING):
        load(part).start()

    barrier = pltpu.get_barrier_semaphore()
    for step in range(RING):
        @pl.when((core == 0) | (step > 0))
        def _():
            pl.semaphore_signal(
                barrier, inc=1, device_id=ring(lax.rem(me + step, RING), 1), device_id_type=MESH)

    @pl.when(core == 1)
    def _():
        for step in range(RING):
            pl.semaphore_signal(
                barrier, inc=1, device_id=ring(lax.rem(me + step, RING), 0), device_id_type=MESH)
        for step in (1, -1):
            pl.semaphore_signal(barrier, inc=1, device_id=beside(step), device_id_type=MESH)

    def share(half, place):
        return pltpu.make_async_remote_copy(
            src_ref=coeffs.at[half, place], dst_ref=parts.at[half, side, core * POD + rep],
            send_sem=rs_send, recv_sem=rs_recv.at[half, side],
            device_id=ring(place, 1), device_id_type=MESH)

    def swap(half, pod):
        return pltpu.make_async_remote_copy(
            src_ref=sums.at[half, pod], dst_ref=around.at[half, pod],
            send_sem=swap_send.at[half, pod], recv_sem=swap_recv.at[half, pod],
            device_id=beside(2 * pod - 1), device_id_type=MESH)

    def spread(half, to_core, place):
        return pltpu.make_async_remote_copy(
            src_ref=mixed.at[half, place // POD, to_core], dst_ref=got.at[half, me],
            send_sem=ag_send, recv_sem=ag_recv.at[half],
            device_id=ring(place, to_core), device_id_type=MESH)

    def bytes_of(blocks, sem):
        return pltpu.make_async_copy(parts.at[0, 0, pl.ds(0, blocks)], parts.at[0, 0, pl.ds(0, blocks)], sem)

    table_copy.wait()
    set_up(table, enc_cols, enc_rows, dec_cols, dec_rows)

    for half in range(2):
        for part in range(4):
            load(half * 4 + part).wait()
        groups = [x[:, pl.ds((half * RING + g) * wide, wide)] for g in range(RING)]
        out = encode(groups, enc_cols, enc_rows)
        for g in range(RING):
            coeffs[half, g] = out[:, g * 128:(g + 1) * 128]

    @pl.when(core == 0)
    def _():
        pl.semaphore_wait(barrier, RING)

    @pl.when(core == 1)
    def _():
        pl.semaphore_wait(barrier, 2 * RING + 1)
        for half in range(2):
            parts[half, side, POD + rep] = coeffs[half, me]

    for half in range(2):
        @pl.loop(0, RING - core)
        def _(step):
            share(half, place_at(step)).start()

    def put_fresh(g, value):
        cols = pl.ds(g * wide, wide)
        fresh[0, 0, :, cols] = x[:, cols] - value

    decode([coeffs[half, g] for half in range(2) for g in range(RING)], dec_cols, dec_rows, put_fresh)

    @pl.when(core == 1)
    def _():
        for half in range(2):
            for pod, blocks in ((side, RING - 1), (1 - side, RING)):
                bytes_of(blocks, rs_recv.at[half, pod]).wait()
                for of_core in range(2):
                    terms = [parts[half, pod, of_core * POD + r] for r in range(POD)]
                    sums[half, pod, of_core] = (terms[0] + terms[1]) + (terms[2] + terms[3])
                swap(half, pod).start()

        for half in range(2):
            for pod in range(2):
                swap(half, pod).wait_recv()
            for pod in range(2):
                mixed[half, pod] = 0.5 * sums[half, pod] + 0.25 * (sums[half, 1 - pod] + around[half, 1 - pod])
            for to_core in range(2):
                @pl.loop(0, RING - to_core)
                def _(step):
                    spread(half, to_core, place_at(step)).start()
            got[half, me] = mixed[half, side, 1]

        for half in range(2):
            bytes_of(RING - 1, rs_send).wait()
            for pod in range(2):
                swap(half, pod).wait_send()

    @pl.when(core == 0)
    def _():
        for half in range(2):
            bytes_of(RING, rs_send).wait()

    for half in range(2):
        @pl.when(core == 0)
        def _():
            bytes_of(RING, ag_recv.at[half]).wait()

        @pl.when(core == 1)
        def _():
            bytes_of(RING - 1, ag_recv.at[half]).wait()

        def put_update(g, value):
            update[0, :, pl.ds((half * RING + g) * wide, wide)] = value.astype(BF16)

        decode([got[half, g] for g in range(RING)], dec_cols, dec_rows, put_update)

    @pl.when(core == 1)
    def _():
        for half in range(2):
            for to_core in range(2):
                bytes_of(RING - to_core, ag_send).wait()


def write_out(fresh_in, update_in, fresh, update, sems):
    copies = [pltpu.make_async_copy(fresh_in, fresh, sems.at[0]), pltpu.make_async_copy(update_in, update, sems.at[1])]
    for copy in copies:
        copy.start()
    for copy in copies:
        copy.wait()


def local(momentum):
    rows, cols = momentum.shape[2:]
    table = jnp.asarray(tables())
    vmem = pl.BlockSpec(memory_space=pltpu.VMEM)
    anywhere = pl.BlockSpec(memory_space=pl.ANY)
    block = (KEEP, GROUP * KEEP)
    dma = pltpu.SemaphoreType.DMA
    fresh, update = pl.pallas_call(
        kernel,
        out_shape=(
            pltpu.VMEM(momentum.shape, F32),
            pltpu.VMEM((1, rows, cols), BF16),
        ),
        in_specs=[pl.BlockSpec(memory_space=pltpu.HBM)] * 2,
        out_specs=(vmem, vmem),
        scratch_shapes=[
            pltpu.VMEM((rows, cols), F32),
            pltpu.VMEM(table.shape, F32),
            pltpu.VMEM((512, 256), BF16),
            pltpu.VMEM((16, 192), BF16),
            pltpu.VMEM((384, 512), BF16),
            pltpu.VMEM((64, 48), BF16),
            pltpu.VMEM((2, RING, *block), F32),
            pltpu.VMEM((2, 2, RING, *block), F32),
            pltpu.VMEM((2, 2, 2, *block), F32),
            pltpu.VMEM((2, 2, 2, *block), F32),
            pltpu.VMEM((2, 2, 2, *block), F32),
            pltpu.VMEM((2, RING, *block), F32),
            dma((RING,)),
            dma,
            dma,
            dma((2, 2)),
            dma((2, 2)),
            dma((2, 2)),
            dma,
            dma((2,)),
        ],
        compiler_params=pltpu.CompilerParams(
            collective_id=0, has_side_effects=True, vmem_limit_bytes=60 * 1024 * 1024),
    )(momentum, table)
    return pl.pallas_call(
        write_out,
        out_shape=(jax.ShapeDtypeStruct(fresh.shape, F32), jax.ShapeDtypeStruct(update.shape, BF16)),
        in_specs=[anywhere] * 2,
        out_specs=(anywhere,) * 2,
        scratch_shapes=[dma((2,))],
        compiler_params=pltpu.CompilerParams(vmem_limit_bytes=8 * 1024 * 1024),
    )(fresh, update)


def solution(mesh):
    in_specs = (P("outer", "rep", "shard", None),)
    out_specs = (P("outer", "rep", "shard", None), P("outer", "shard", None))
    return jax.shard_map(local, mesh=mesh, in_specs=in_specs, out_specs=out_specs, check_vma=False)
```

time: 26.8 us -> 23.8 us (0.89)
  the two profiles are of different devices: /device:TPU:384 before, /device:TPU:1 now
where the time goes in v2:
time: 23.8 us; the launch traced here: 23.5 us
  Pallas kernels  22.9 us (96%)
  between operations  0.64 us (3%)
    pallas_call x1, Pallas kernels, local(): pl.pallas_call(kernel, out_shape=(pltpu.VMEM(momentum.shape, F32), pltpu....  21.2 us
    pallas_call x1, Pallas kernels, local(): pl.pallas_call(write_out, out_shape=(jax.ShapeDtypeStruct(fresh.shape, F3...  1.68 us

profile of v2, /device:TPU:1, one launch (start us, length us, event | category | flops | bytes accessed | tf_op | source)
XLA Modules:
  0.0 23.5 jit_solution(14784146649743616739)
XLA Ops:
  0.6 21.2 %shard_map.41 = (f32[1,1,64,8192]{3,2,1,0:T(8,128)S(1)}, bf16[1,64,8192]{2,1,0:T(8,128)(2,1)S(1)}) custom-call(f32[1,1,64,8192]{3,2,1,0:T(8,128)} %x_hbm.1, f32[208,256]{1,0:T(8,128)} %constant.2.clone.table_hbm), custom_call_target="tpu_custom_call" | custom-call | tf_op jit(solution)/shard_map/pallas_call | solution.py:253
  21.8 1.7 %shard_map.42 = (f32[1,1,64,8192]{3,2,1,0:T(8,128)}, bf16[1,64,8192]{2,1,0:T(8,128)(2,1)}) custom-call(f32[1,1,64,8192]{3,2,1,0:T(8,128)S(1)} %get-tuple-element.4.fresh_in, bf16[1,64,8192]{2,1,0:T(8,128)(2,1)S(1)} %get-tuple-element.5.update_in), custom_call_target="tpu_custom_call" | custom-call | tf_op jit(solution)/shard_map/pallas_call | solution.py:286

commit v3 on v2

--- a/solution.py
+++ b/solution.py
@@ -14,7 +14,7 @@
 RING = 8
 POD = 4
 GROUP = 8
-MESH = pl.DeviceIdType.MESH
+LOGICAL = pl.DeviceIdType.LOGICAL
 BF16 = jnp.bfloat16
 F32 = jnp.float32
 
@@ -87,8 +87,8 @@
         put(g, dot(dec_rows[...], jnp.concatenate([high, low, high], axis=0)))
 
 
-def kernel(x_hbm, table_hbm, fresh, update,
-           x, table, enc_cols, enc_rows, dec_cols, dec_rows, coeffs, parts, sums, around, mixed, got,
+def kernel(x_hbm, table_hbm, fresh, update, later, dec_cols, dec_rows,
+           x, table, enc_cols, enc_rows, coeffs, parts, sums, around, mixed, got,
            x_sem, table_sem, rs_send, rs_recv, swap_send, swap_recv, ag_send, ag_recv):
     outer, rep, shard = (lax.axis_index(axis) for axis in ("outer", "rep", "shard"))
     columns = lax.axis_size("outer") // 2
@@ -96,15 +96,15 @@
     me = side * POD + rep
     wide = GROUP * TILE
 
-    def ring(place, to_core):
-        return {"outer": column * 2 + place // POD, "rep": place % POD, "shard": shard - core + to_core}
-
-    def beside(step):
-        return {"outer": lax.rem(column + step + columns, columns) * 2 + side}
-
-    def place_at(step):
-        half = (step + 1) // 2
-        return lax.rem(me + 4 + half * (1 - 2 * (step % 2)), RING)
+    places = [lax.rem(me + ahead, RING) for ahead in (4, 3, 5, 2, 6, 1, 7, 0)]
+    n_shard = lax.axis_size("shard")
+    here = shard - core
+    targets = [((column * 2 + place // POD) * POD + place % POD) * n_shard + here for place in places]
+    pods = [place // POD for place in places]
+
+    def beside(pod):
+        to = lax.rem(column + 2 * pod - 1 + columns, columns)
+        return ((to * 2 + side) * POD + rep) * n_shard + here + 1
 
     def load(part):
         cols = pl.ds(part * 2 * wide, 2 * wide)
@@ -116,37 +116,41 @@
         load(part).start()
 
     barrier = pltpu.get_barrier_semaphore()
-    for step in range(RING):
-        @pl.when((core == 0) | (step > 0))
-        def _():
-            pl.semaphore_signal(
-                barrier, inc=1, device_id=ring(lax.rem(me + step, RING), 1), device_id_type=MESH)
+
+    def signal(device):
+        pl.semaphore_signal(barrier, inc=1, device_id=device, device_id_type=LOGICAL)
+
+    for target in targets[:-1]:
+        signal(target + 1)
+
+    @pl.when(core == 0)
+    def _():
+        signal(targets[-1] + 1)
 
     @pl.when(core == 1)
     def _():
-        for step in range(RING):
-            pl.semaphore_signal(
-                barrier, inc=1, device_id=ring(lax.rem(me + step, RING), 0), device_id_type=MESH)
-        for step in (1, -1):
-            pl.semaphore_signal(barrier, inc=1, device_id=beside(step), device_id_type=MESH)
-
-    def share(half, place):
+        for target in targets:
+            signal(target)
+        for pod in range(2):
+            signal(beside(pod))
+
+    def share(half, step):
         return pltpu.make_async_remote_copy(
-            src_ref=coeffs.at[half, place], dst_ref=parts.at[half, side, core * POD + rep],
+            src_ref=coeffs.at[half, places[step]], dst_ref=parts.at[half, side, core * POD + rep],
             send_sem=rs_send, recv_sem=rs_recv.at[half, side],
-            device_id=ring(place, 1), device_id_type=MESH)
+            device_id=targets[step] + 1, device_id_type=LOGICAL)
 
     def swap(half, pod):
         return pltpu.make_async_remote_copy(
             src_ref=sums.at[half, pod], dst_ref=around.at[half, pod],
             send_sem=swap_send.at[half, pod], recv_sem=swap_recv.at[half, pod],
-            device_id=beside(2 * pod - 1), device_id_type=MESH)
-
-    def spread(half, to_core, place):
+            device_id=beside(pod), device_id_type=LOGICAL)
+
+    def spread(half, to_core, step):
         return pltpu.make_async_remote_copy(
-            src_ref=mixed.at[half, place // POD, to_core], dst_ref=got.at[half, me],
+            src_ref=mixed.at[half, pods[step], to_core], dst_ref=got.at[half, me],
             send_sem=ag_send, recv_sem=ag_recv.at[half],
-            device_id=ring(place, to_core), device_id_type=MESH)
+            device_id=targets[step] + to_core, device_id_type=LOGICAL)
 
     def bytes_of(blocks, sem):
         return pltpu.make_async_copy(parts.at[0, 0, pl.ds(0, blocks)], parts.at[0, 0, pl.ds(0, blocks)], sem)
@@ -162,20 +166,25 @@
         for g in range(RING):
             coeffs[half, g] = out[:, g * 128:(g + 1) * 128]
 
-    @pl.when(core == 0)
-    def _():
-        pl.semaphore_wait(barrier, RING)
-
-    @pl.when(core == 1)
-    def _():
-        pl.semaphore_wait(barrier, 2 * RING + 1)
-        for half in range(2):
+        if half == 0:
+            @pl.when(core == 0)
+            def _():
+                pl.semaphore_wait(barrier, RING)
+
+            @pl.when(core == 1)
+            def _():
+                pl.semaphore_wait(barrier, 2 * RING + 1)
+
+        for step in range(RING - 1):
+            share(half, step).start()
+
+        @pl.when(core == 0)
+        def _():
+            share(half, RING - 1).start()
+
+        @pl.when(core == 1)
+        def _():
             parts[half, side, POD + rep] = coeffs[half, me]
-
-    for half in range(2):
-        @pl.loop(0, RING - core)
-        def _(step):
-            share(half, place_at(step)).start()
 
     def put_fresh(g, value):
         cols = pl.ds(g * wide, wide)
@@ -199,9 +208,8 @@
             for pod in range(2):
                 mixed[half, pod] = 0.5 * sums[half, pod] + 0.25 * (sums[half, 1 - pod] + around[half, 1 - pod])
             for to_core in range(2):
-                @pl.loop(0, RING - to_core)
-                def _(step):
-                    spread(half, to_core, place_at(step)).start()
+                for step in range(RING - to_core):
+                    spread(half, to_core, step).start()
             got[half, me] = mixed[half, side, 1]
 
         for half in range(2):
@@ -223,10 +231,13 @@
         def _():
             bytes_of(RING - 1, ag_recv.at[half]).wait()
 
-        def put_update(g, value):
-            update[0, :, pl.ds((half * RING + g) * wide, wide)] = value.astype(BF16)
-
-        decode([got[half, g] for g in range(RING)], dec_cols, dec_rows, put_update)
+        if half == 0:
+            def put_update(g, value):
+                update[:, pl.ds(g * wide, wide)] = value.astype(BF16)
+
+            decode([got[0, g] for g in range(RING)], dec_cols, dec_rows, put_update)
+        else:
+            later[...] = got[1]
 
     @pl.when(core == 1)
     def _():
@@ -235,10 +246,21 @@
                 bytes_of(RING - to_core, ag_send).wait()
 
 
-def write_out(fresh_in, update_in, fresh, update, sems):
-    copies = [pltpu.make_async_copy(fresh_in, fresh, sems.at[0]), pltpu.make_async_copy(update_in, update, sems.at[1])]
+def finish(fresh_in, update_in, later, dec_cols, dec_rows, fresh, update, second, sems):
+    half = second.shape[1]
+    copies = [
+        pltpu.make_async_copy(fresh_in, fresh, sems.at[0]),
+        pltpu.make_async_copy(update_in, update.at[0, :, pl.ds(0, half)], sems.at[1]),
+    ]
     for copy in copies:
         copy.start()
+
+    def put(g, value):
+        second[:, pl.ds(g * GROUP * TILE, GROUP * TILE)] = value.astype(BF16)
+
+    decode([later[g] for g in range(RING)], dec_cols, dec_rows, put)
+    copies.append(pltpu.make_async_copy(second, update.at[0, :, pl.ds(half, half)], sems.at[2]))
+    copies[-1].start()
     for copy in copies:
         copy.wait()
 
@@ -250,21 +272,22 @@
     anywhere = pl.BlockSpec(memory_space=pl.ANY)
     block = (KEEP, GROUP * KEEP)
     dma = pltpu.SemaphoreType.DMA
-    fresh, update = pl.pallas_call(
+    fresh, *rest = pl.pallas_call(
         kernel,
         out_shape=(
             pltpu.VMEM(momentum.shape, F32),
-            pltpu.VMEM((1, rows, cols), BF16),
+            pltpu.VMEM((rows, cols // 2), BF16),
+            pltpu.VMEM((RING, *block), F32),
+            pltpu.VMEM((384, 512), BF16),
+            pltpu.VMEM((64, 48), BF16),
         ),
         in_specs=[pl.BlockSpec(memory_space=pltpu.HBM)] * 2,
-        out_specs=(vmem, vmem),
+        out_specs=(vmem,) * 5,
         scratch_shapes=[
             pltpu.VMEM((rows, cols), F32),
             pltpu.VMEM(table.shape, F32),
             pltpu.VMEM((512, 256), BF16),
             pltpu.VMEM((16, 192), BF16),
-            pltpu.VMEM((384, 512), BF16),
-            pltpu.VMEM((64, 48), BF16),
             pltpu.VMEM((2, RING, *block), F32),
             pltpu.VMEM((2, 2, RING, *block), F32),
             pltpu.VMEM((2, 2, 2, *block), F32),
@@ -284,13 +307,13 @@
             collective_id=0, has_side_effects=True, vmem_limit_bytes=60 * 1024 * 1024),
     )(momentum, table)
     return pl.pallas_call(
-        write_out,
-        out_shape=(jax.ShapeDtypeStruct(fresh.shape, F32), jax.ShapeDtypeStruct(update.shape, BF16)),
-        in_specs=[anywhere] * 2,
+        finish,
+        out_shape=(jax.ShapeDtypeStruct(fresh.shape, F32), jax.ShapeDtypeStruct((1, rows, cols), BF16)),
+        in_specs=[anywhere] * 2 + [vmem] * 3,
         out_specs=(anywhere,) * 2,
-        scratch_shapes=[dma((2,))],
-        compiler_params=pltpu.CompilerParams(vmem_limit_bytes=8 * 1024 * 1024),
-    )(fresh, update)
+        scratch_shapes=[pltpu.VMEM((rows, cols // 2), BF16), dma((3,))],
+        compiler_params=pltpu.CompilerParams(vmem_limit_bytes=16 * 1024 * 1024),
+    )(fresh, *rest)
 
 
 def solution(mesh):

time: 23.8 us -> 23.3 us (0.979)
  Pallas kernels: 22.9 us -> 22.5 us
    pallas_call x1, Pallas kernels: 21.2 us -> 20.8 us  [local(): pl.pallas_call(kernel, out_shape=(pltpu.VMEM(momentum.shape, F32), pltpu....]
where the time goes in v3:
time: 23.3 us; the launch traced here: 23.2 us
  Pallas kernels  22.5 us (97%)
  between operations  0.64 us (3%)
    pallas_call x1, Pallas kernels, local(): pl.pallas_call(kernel, out_shape=(pltpu.VMEM(momentum.shape, F32), pltpu....  20.8 us
    pallas_call x1, Pallas kernels, local(): pl.pallas_call(finish, out_shape=(jax.ShapeDtypeStruct(fresh.shape, F32),...  1.69 us

profile of v3, /device:TPU:1, one launch (start us, length us, event | category | flops | bytes accessed | tf_op | source)
XLA Modules:
  0.0 23.2 jit_solution(11674016440460417303)
XLA Ops:
  0.6 20.8 %shard_map.41 = (f32[1,1,64,8192]{3,2,1,0:T(8,128)S(1)}, bf16[64,4096]{1,0:T(8,128)(2,1)S(1)}, f32[8,16,128]{2,1,0:T(8,128)S(1)}, bf16[384,512]{1,0:T(8,128)(2,1)S(1)}, bf16[64,48]{1,0:T(8,128)(2,1)S(1)}) custom-call(f32[1,1,64,8192]{3,2,1,0:T(8,128)} %x_hbm.1, f32[208,256]{1,0:T(8,128)} %constant.2.clone.table_hbm), custom_call_target="tpu_custom_call" | custom-call | tf_op jit(solution)/shard_map/pallas_call | solution.py:275
  21.5 1.7 %shard_map.42 = (f32[1,1,64,8192]{3,2,1,0:T(8,128)}, bf16[1,64,8192]{2,1,0:T(8,128)(2,1)}) custom-call(f32[1,1,64,8192]{3,2,1,0:T(8,128)S(1)} %get-tuple-element.7.fresh_in, bf16[64,4096]{1,0:T(8,128)(2,1)S(1)} %get-tuple-element.8.update_in, f32[8,16,128]{2,1,0:T(8,128)S(1)} %get-tuple-element.9.later, bf16[384,512]{1,0:T(8,128)(2,1)S(1)} %get-tuple-element.10.dec_cols, ...), custom_call_target="tpu_custom_call" | custom-call | tf_op jit(solution)/shard_map/pallas_call | solution.py:309

commit v4 on v3

--- a/solution.py
+++ b/solution.py
@@ -44,19 +44,26 @@
     return out
 
 
-def set_up(table, enc_cols, enc_rows, dec_cols, dec_rows):
+def encode_operands(table, enc_cols, enc_rows):
+    row = lax.broadcasted_iota(jnp.int32, (128, 128), 0)
+    col = lax.broadcasted_iota(jnp.int32, (128, 128), 1)
     for place in range(4):
         lanes = pl.ds(place * 128, 128)
-        row = lax.broadcasted_iota(jnp.int32, (128, 128), 0)
-        col = lax.broadcasted_iota(jnp.int32, (128, 128), 1)
+        high, low = split(jnp.where(col // KEEP == 2 * place + row // TILE, table[:128, 128:], 0.0))
+        enc_cols[lanes, :128] = high
+        enc_cols[lanes, 128:] = low
+    enc_rows[...] = table[128:144, :192].astype(BF16)
+
+
+def decode_operands(table, dec_cols, dec_rows):
+    row = lax.broadcasted_iota(jnp.int32, (128, 128), 0)
+    col = lax.broadcasted_iota(jnp.int32, (128, 128), 1)
+    for place in range(4):
+        lanes = pl.ds(place * 128, 128)
         high, low = split(jnp.where(row // KEEP == 2 * place + col // TILE, table[:128, :128], 0.0))
         dec_cols[:128, lanes] = high
         dec_cols[128:256, lanes] = high
         dec_cols[256:, lanes] = low
-        high, low = split(jnp.where(col // KEEP == 2 * place + row // TILE, table[:128, 128:], 0.0))
-        enc_cols[lanes, :128] = high
-        enc_cols[lanes, 128:] = low
-    enc_rows[...] = table[128:144, :192].astype(BF16)
     dec_rows[...] = table[144:, :48].astype(BF16)
 
 
@@ -96,11 +103,14 @@
     me = side * POD + rep
     wide = GROUP * TILE
 
-    places = [lax.rem(me + ahead, RING) for ahead in (4, 3, 5, 2, 6, 1, 7, 0)]
     n_shard = lax.axis_size("shard")
     here = shard - core
-    targets = [((column * 2 + place // POD) * POD + place % POD) * n_shard + here for place in places]
-    pods = [place // POD for place in places]
+
+    def target(place):
+        return ((column * 2 + place // POD) * POD + place % POD) * n_shard + here
+
+    places = [lax.rem(me + ahead, RING) for ahead in (4, 3, 5, 2, 6, 1, 7, 0)]
+    targets = [target(place) for place in places]
 
     def beside(pod):
         to = lax.rem(column + 2 * pod - 1 + columns, columns)
@@ -120,8 +130,8 @@
     def signal(device):
         pl.semaphore_signal(barrier, inc=1, device_id=device, device_id_type=LOGICAL)
 
-    for target in targets[:-1]:
-        signal(target + 1)
+    for device in targets[:-1]:
+        signal(device + 1)
 
     @pl.when(core == 0)
     def _():
@@ -129,34 +139,36 @@
 
     @pl.when(core == 1)
     def _():
-        for target in targets:
-            signal(target)
+        for device in targets:
+            signal(device)
         for pod in range(2):
             signal(beside(pod))
 
     def share(half, step):
         return pltpu.make_async_remote_copy(
-            src_ref=coeffs.at[half, places[step]], dst_ref=parts.at[half, side, core * POD + rep],
-            send_sem=rs_send, recv_sem=rs_recv.at[half, side],
+            src_ref=coeffs.at[half, places[step]], dst_ref=parts.at[half, core, side, rep],
+            send_sem=rs_send, recv_sem=rs_recv.at[half, core, side],
             device_id=targets[step] + 1, device_id_type=LOGICAL)
 
-    def swap(half, pod):
+    def swap(half, of_core, pod):
         return pltpu.make_async_remote_copy(
-            src_ref=sums.at[half, pod], dst_ref=around.at[half, pod],
-            send_sem=swap_send.at[half, pod], recv_sem=swap_recv.at[half, pod],
+            src_ref=sums.at[half, of_core, pod], dst_ref=around.at[half, of_core, pod],
+            send_sem=swap_send, recv_sem=swap_recv.at[half, of_core, pod],
             device_id=beside(pod), device_id_type=LOGICAL)
 
-    def spread(half, to_core, step):
+    def spread(half, to_core, pod, ahead):
+        place = pod * POD + lax.rem(rep + ahead, POD)
         return pltpu.make_async_remote_copy(
-            src_ref=mixed.at[half, pods[step], to_core], dst_ref=got.at[half, me],
+            src_ref=mixed.at[half, to_core, pod], dst_ref=got.at[half, me],
             send_sem=ag_send, recv_sem=ag_recv.at[half],
-            device_id=targets[step] + to_core, device_id_type=LOGICAL)
+            device_id=target(place) + to_core, device_id_type=LOGICAL)
 
     def bytes_of(blocks, sem):
-        return pltpu.make_async_copy(parts.at[0, 0, pl.ds(0, blocks)], parts.at[0, 0, pl.ds(0, blocks)], sem)
+        some = coeffs.at[0, pl.ds(0, blocks)]
+        return pltpu.make_async_copy(some, some, sem)
 
     table_copy.wait()
-    set_up(table, enc_cols, enc_rows, dec_cols, dec_rows)
+    encode_operands(table, enc_cols, enc_rows)
 
     for half in range(2):
         for part in range(4):
@@ -184,38 +196,48 @@
 
         @pl.when(core == 1)
         def _():
-            parts[half, side, POD + rep] = coeffs[half, me]
+            parts[half, 1, side, rep] = coeffs[half, me]
 
     def put_fresh(g, value):
         cols = pl.ds(g * wide, wide)
         fresh[0, 0, :, cols] = x[:, cols] - value
 
+    decode_operands(table, dec_cols, dec_rows)
     decode([coeffs[half, g] for half in range(2) for g in range(RING)], dec_cols, dec_rows, put_fresh)
 
     @pl.when(core == 1)
     def _():
         for half in range(2):
-            for pod, blocks in ((side, RING - 1), (1 - side, RING)):
-                bytes_of(blocks, rs_recv.at[half, pod]).wait()
-                for of_core in range(2):
-                    terms = [parts[half, pod, of_core * POD + r] for r in range(POD)]
-                    sums[half, pod, of_core] = (terms[0] + terms[1]) + (terms[2] + terms[3])
-                swap(half, pod).start()
-
-        for half in range(2):
-            for pod in range(2):
-                swap(half, pod).wait_recv()
-            for pod in range(2):
-                mixed[half, pod] = 0.5 * sums[half, pod] + 0.25 * (sums[half, 1 - pod] + around[half, 1 - pod])
-            for to_core in range(2):
-                for step in range(RING - to_core):
-                    spread(half, to_core, step).start()
-            got[half, me] = mixed[half, side, 1]
+            for of_core in (1, 0):
+                for pod, own in ((side, 1), (1 - side, 0)):
+                    bytes_of(POD - own * of_core, rs_recv.at[half, of_core, pod]).wait()
+                    terms = [parts[half, of_core, pod, r] for r in range(POD)]
+                    sums[half, of_core, pod] = (terms[0] + terms[1]) + (terms[2] + terms[3])
+                    swap(half, of_core, pod).start()
+
+        for half in range(2):
+            for of_core in (1, 0):
+                for pod in range(2):
+                    swap(half, of_core, 1 - pod).wait_recv()
+                    mixed[half, of_core, pod] = 0.5 * sums[half, of_core, pod] + 0.25 * (
+                        sums[half, of_core, 1 - pod] + around[half, of_core, 1 - pod])
+                    if of_core == 0:
+                        spread(half, of_core, pod, 0).start()
+                    else:
+                        @pl.when(pod != side)
+                        def _():
+                            spread(half, of_core, pod, 0).start()
+
+                        @pl.when(pod == side)
+                        def _():
+                            got[half, me] = mixed[half, of_core, pod]
+
+                    for ahead in range(1, POD):
+                        spread(half, of_core, pod, ahead).start()
 
         for half in range(2):
             bytes_of(RING - 1, rs_send).wait()
-            for pod in range(2):
-                swap(half, pod).wait_send()
+        bytes_of(RING, swap_send).wait()
 
     @pl.when(core == 0)
     def _():
@@ -289,7 +311,7 @@
             pltpu.VMEM((512, 256), BF16),
             pltpu.VMEM((16, 192), BF16),
             pltpu.VMEM((2, RING, *block), F32),
-            pltpu.VMEM((2, 2, RING, *block), F32),
+            pltpu.VMEM((2, 2, 2, POD, *block), F32),
             pltpu.VMEM((2, 2, 2, *block), F32),
             pltpu.VMEM((2, 2, 2, *block), F32),
             pltpu.VMEM((2, 2, 2, *block), F32),
@@ -297,9 +319,9 @@
             dma((RING,)),
             dma,
             dma,
-            dma((2, 2)),
-            dma((2, 2)),
-            dma((2, 2)),
+            dma((2, 2, 2)),
+            dma,
+            dma((2, 2, 2)),
             dma,
             dma((2,)),
         ],

time: 23.3 us -> 22.5 us (0.966)
  Pallas kernels: 22.5 us -> 21.6 us
    pallas_call x1, Pallas kernels: 20.8 us -> 19.9 us  [local(): pl.pallas_call(kernel, out_shape=(pltpu.VMEM(momentum.shape, F32), pltpu....]
where the time goes in v4:
time: 22.5 us; the launch traced here: 22.2 us
  Pallas kernels  21.6 us (96%)
  between operations  0.64 us (3%)
    pallas_call x1, Pallas kernels, local(): pl.pallas_call(kernel, out_shape=(pltpu.VMEM(momentum.shape, F32), pltpu....  19.9 us
    pallas_call x1, Pallas kernels, local(): pl.pallas_call(finish, out_shape=(jax.ShapeDtypeStruct(fresh.shape, F32),...  1.69 us

profile of v4, /device:TPU:1, one launch (start us, length us, event | category | flops | bytes accessed | tf_op | source)
XLA Modules:
  0.0 22.2 jit_solution(696737261494983232)
XLA Ops:
  0.6 19.9 %shard_map.41 = (f32[1,1,64,8192]{3,2,1,0:T(8,128)S(1)}, bf16[64,4096]{1,0:T(8,128)(2,1)S(1)}, f32[8,16,128]{2,1,0:T(8,128)S(1)}, bf16[384,512]{1,0:T(8,128)(2,1)S(1)}, bf16[64,48]{1,0:T(8,128)(2,1)S(1)}) custom-call(f32[1,1,64,8192]{3,2,1,0:T(8,128)} %x_hbm.1, f32[208,256]{1,0:T(8,128)} %constant.2.clone.table_hbm), custom_call_target="tpu_custom_call" | custom-call | tf_op jit(solution)/shard_map/pallas_call | solution.py:297
  20.5 1.7 %shard_map.42 = (f32[1,1,64,8192]{3,2,1,0:T(8,128)}, bf16[1,64,8192]{2,1,0:T(8,128)(2,1)}) custom-call(f32[1,1,64,8192]{3,2,1,0:T(8,128)S(1)} %get-tuple-element.7.fresh_in, bf16[64,4096]{1,0:T(8,128)(2,1)S(1)} %get-tuple-element.8.update_in, f32[8,16,128]{2,1,0:T(8,128)S(1)} %get-tuple-element.9.later, bf16[384,512]{1,0:T(8,128)(2,1)S(1)} %get-tuple-element.10.dec_cols, ...), custom_call_target="tpu_custom_call" | custom-call | tf_op jit(solution)/shard_map/pallas_call | solution.py:331

commit v5 on v4

--- a/solution.py
+++ b/solution.py
@@ -130,17 +130,12 @@
     def signal(device):
         pl.semaphore_signal(barrier, inc=1, device_id=device, device_id_type=LOGICAL)
 
-    for device in targets[:-1]:
-        signal(device + 1)
-
-    @pl.when(core == 0)
-    def _():
-        signal(targets[-1] + 1)
-
     @pl.when(core == 1)
     def _():
-        for device in targets:
+        for device in targets[:-1]:
             signal(device)
+            signal(device + 1)
+        signal(targets[-1])
         for pod in range(2):
             signal(beside(pod))
 
@@ -185,7 +180,7 @@
 
             @pl.when(core == 1)
             def _():
-                pl.semaphore_wait(barrier, 2 * RING + 1)
+                pl.semaphore_wait(barrier, RING + 1)
 
         for step in range(RING - 1):
             share(half, step).start()

time: 22.5 us -> 22 us (0.978)
  Pallas kernels: 21.6 us -> 21.2 us
    pallas_call x1, Pallas kernels: 19.9 us -> 19.5 us  [local(): pl.pallas_call(kernel, out_shape=(pltpu.VMEM(momentum.shape, F32), pltpu....]
where the time goes in v5:
time: 22 us; the launch traced here: 21.9 us
  Pallas kernels  21.2 us (96%)
  between operations  0.64 us (3%)
    pallas_call x1, Pallas kernels, local(): pl.pallas_call(kernel, out_shape=(pltpu.VMEM(momentum.shape, F32), pltpu....  19.5 us
    pallas_call x1, Pallas kernels, local(): pl.pallas_call(finish, out_shape=(jax.ShapeDtypeStruct(fresh.shape, F32),...  1.69 us

profile of v5, /device:TPU:1, one launch (start us, length us, event | category | flops | bytes accessed | tf_op | source)
XLA Modules:
  0.0 21.9 jit_solution(2455622895968282718)
XLA Ops:
  0.6 19.5 %shard_map.41 = (f32[1,1,64,8192]{3,2,1,0:T(8,128)S(1)}, bf16[64,4096]{1,0:T(8,128)(2,1)S(1)}, f32[8,16,128]{2,1,0:T(8,128)S(1)}, bf16[384,512]{1,0:T(8,128)(2,1)S(1)}, bf16[64,48]{1,0:T(8,128)(2,1)S(1)}) custom-call(f32[1,1,64,8192]{3,2,1,0:T(8,128)} %x_hbm.1, f32[208,256]{1,0:T(8,128)} %constant.2.clone.table_hbm), custom_call_target="tpu_custom_call" | custom-call | tf_op jit(solution)/shard_map/pallas_call | solution.py:292
  20.2 1.7 %shard_map.42 = (f32[1,1,64,8192]{3,2,1,0:T(8,128)}, bf16[1,64,8192]{2,1,0:T(8,128)(2,1)}) custom-call(f32[1,1,64,8192]{3,2,1,0:T(8,128)S(1)} %get-tuple-element.7.fresh_in, bf16[64,4096]{1,0:T(8,128)(2,1)S(1)} %get-tuple-element.8.update_in, f32[8,16,128]{2,1,0:T(8,128)S(1)} %get-tuple-element.9.later, bf16[384,512]{1,0:T(8,128)(2,1)S(1)} %get-tuple-element.10.dec_cols, ...), custom_call_target="tpu_custom_call" | custom-call | tf_op jit(solution)/shard_map/pallas_call | solution.py:326

commit v6 on v5

--- a/solution.py
+++ b/solution.py
@@ -94,7 +94,7 @@
         put(g, dot(dec_rows[...], jnp.concatenate([high, low, high], axis=0)))
 
 
-def kernel(x_hbm, table_hbm, fresh, update, later, dec_cols, dec_rows,
+def kernel(x_hbm, table_hbm, fresh, later, dec_cols, dec_rows,
            x, table, enc_cols, enc_rows, coeffs, parts, sums, around, mixed, got,
            x_sem, table_sem, rs_send, rs_recv, swap_send, swap_recv, ag_send, ag_recv):
     outer, rep, shard = (lax.axis_index(axis) for axis in ("outer", "rep", "shard"))
@@ -248,13 +248,7 @@
         def _():
             bytes_of(RING - 1, ag_recv.at[half]).wait()
 
-        if half == 0:
-            def put_update(g, value):
-                update[:, pl.ds(g * wide, wide)] = value.astype(BF16)
-
-            decode([got[0, g] for g in range(RING)], dec_cols, dec_rows, put_update)
-        else:
-            later[...] = got[1]
+        later[half] = got[half]
 
     @pl.when(core == 1)
     def _():
@@ -263,21 +257,21 @@
                 bytes_of(RING - to_core, ag_send).wait()
 
 
-def finish(fresh_in, update_in, later, dec_cols, dec_rows, fresh, update, second, sems):
-    half = second.shape[1]
-    copies = [
-        pltpu.make_async_copy(fresh_in, fresh, sems.at[0]),
-        pltpu.make_async_copy(update_in, update.at[0, :, pl.ds(0, half)], sems.at[1]),
-    ]
-    for copy in copies:
-        copy.start()
+def finish(fresh_in, later, dec_cols, dec_rows, fresh, update, whole, sems):
+    half = whole.shape[1] // 2
+    wide = GROUP * TILE
+    copies = [pltpu.make_async_copy(fresh_in, fresh, sems.at[0])]
+    for part in range(2):
+        cols = pl.ds(part * half, half)
+        copies.append(pltpu.make_async_copy(whole.at[:, cols], update.at[0, :, cols], sems.at[1 + part]))
+    copies[0].start()
 
     def put(g, value):
-        second[:, pl.ds(g * GROUP * TILE, GROUP * TILE)] = value.astype(BF16)
-
-    decode([later[g] for g in range(RING)], dec_cols, dec_rows, put)
-    copies.append(pltpu.make_async_copy(second, update.at[0, :, pl.ds(half, half)], sems.at[2]))
-    copies[-1].start()
+        whole[:, pl.ds(g * wide, wide)] = value.astype(BF16)
+        if g % RING == RING - 1:
+            copies[1 + g // RING].start()
+
+    decode([later[part, g] for part in range(2) for g in range(RING)], dec_cols, dec_rows, put)
     for copy in copies:
         copy.wait()
 
@@ -293,13 +287,12 @@
         kernel,
         out_shape=(
             pltpu.VMEM(momentum.shape, F32),
-            pltpu.VMEM((rows, cols // 2), BF16),
-            pltpu.VMEM((RING, *block), F32),
+            pltpu.VMEM((2, RING, *block), F32),
             pltpu.VMEM((384, 512), BF16),
             pltpu.VMEM((64, 48), BF16),
         ),
         in_specs=[pl.BlockSpec(memory_space=pltpu.HBM)] * 2,
-        out_specs=(vmem,) * 5,
+        out_specs=(vmem,) * 4,
         scratch_shapes=[
             pltpu.VMEM((rows, cols), F32),
             pltpu.VMEM(table.shape, F32),
@@ -326,9 +319,9 @@
     return pl.pallas_call(
         finish,
         out_shape=(jax.ShapeDtypeStruct(fresh.shape, F32), jax.ShapeDtypeStruct((1, rows, cols), BF16)),
-        in_specs=[anywhere] * 2 + [vmem] * 3,
+        in_specs=[anywhere] + [vmem] * 3,
         out_specs=(anywhere,) * 2,
-        scratch_shapes=[pltpu.VMEM((rows, cols // 2), BF16), dma((3,))],
+        scratch_shapes=[pltpu.VMEM((rows, cols), BF16), dma((3,))],
         compiler_params=pltpu.CompilerParams(vmem_limit_bytes=16 * 1024 * 1024),
     )(fresh, *rest)
 

time: 22 us -> 22 us (level)
  no operation moved by 1% of the time
where the time goes in v6:
time: 22 us; the launch traced here: 21.9 us
  Pallas kernels  21.2 us (96%)
  between operations  0.64 us (3%)
    pallas_call x1, Pallas kernels, local(): pl.pallas_call(kernel, out_shape=(pltpu.VMEM(momentum.shape, F32), pltpu....  19.5 us
    pallas_call x1, Pallas kernels, local(): pl.pallas_call(finish, out_shape=(jax.ShapeDtypeStruct(fresh.shape, F32),...  1.69 us

profile of v6, /device:TPU:1, one launch (start us, length us, event | category | flops | bytes accessed | tf_op | source)
XLA Modules:
  0.0 21.9 jit_solution(8775158053747272663)
XLA Ops:
  0.6 19.5 %shard_map.41 = (f32[1,1,64,8192]{3,2,1,0:T(8,128)S(1)}, f32[2,8,16,128]{3,2,1,0:T(8,128)S(1)}, bf16[384,512]{1,0:T(8,128)(2,1)S(1)}, bf16[64,48]{1,0:T(8,128)(2,1)S(1)}) custom-call(f32[1,1,64,8192]{3,2,1,0:T(8,128)} %x_hbm.1, f32[208,256]{1,0:T(8,128)} %constant.2.clone.table_hbm), custom_call_target="tpu_custom_call" | custom-call | tf_op jit(solution)/shard_map/pallas_call | solution.py:286
  20.2 1.7 %shard_map.42 = (f32[1,1,64,8192]{3,2,1,0:T(8,128)}, bf16[1,64,8192]{2,1,0:T(8,128)(2,1)}) custom-call(f32[1,1,64,8192]{3,2,1,0:T(8,128)S(1)} %get-tuple-element.6.fresh_in, f32[2,8,16,128]{3,2,1,0:T(8,128)S(1)} %get-tuple-element.7.later, bf16[384,512]{1,0:T(8,128)(2,1)S(1)} %get-tuple-element.8.dec_cols, bf16[64,48]{1,0:T(8,128)(2,1)S(1)} %get-tuple-element.9.dec_rows), custom_call_target="tpu_custom_call" | custom-call | tf_op jit(solution)/shard_map/pallas_call | solution.py:319

commit v7 on v6

--- a/solution.py
+++ b/solution.py
@@ -204,8 +204,18 @@
     def _():
         for half in range(2):
             for of_core in (1, 0):
-                for pod, own in ((side, 1), (1 - side, 0)):
-                    bytes_of(POD - own * of_core, rs_recv.at[half, of_core, pod]).wait()
+                for pod in (1, 0):
+                    if of_core == 0:
+                        bytes_of(POD, rs_recv.at[half, of_core, pod]).wait()
+                    else:
+                        @pl.when(pod == side)
+                        def _():
+                            bytes_of(POD - 1, rs_recv.at[half, of_core, pod]).wait()
+
+                        @pl.when(pod != side)
+                        def _():
+                            bytes_of(POD, rs_recv.at[half, of_core, pod]).wait()
+
                     terms = [parts[half, of_core, pod, r] for r in range(POD)]
                     sums[half, of_core, pod] = (terms[0] + terms[1]) + (terms[2] + terms[3])
                     swap(half, of_core, pod).start()

time: 22 us -> 22 us (level)
  no operation moved by 1% of the time
where the time goes in v7:
time: 22 us; the launch traced here: 21.9 us
  Pallas kernels  21.2 us (96%)
  between operations  0.64 us (3%)
    pallas_call x1, Pallas kernels, local(): pl.pallas_call(kernel, out_shape=(pltpu.VMEM(momentum.shape, F32), pltpu....  19.5 us
    pallas_call x1, Pallas kernels, local(): pl.pallas_call(finish, out_shape=(jax.ShapeDtypeStruct(fresh.shape, F32),...  1.69 us

profile of v7, /device:TPU:1, one launch (start us, length us, event | category | flops | bytes accessed | tf_op | source)
XLA Modules:
  0.0 21.9 jit_solution(14080406807306631556)
XLA Ops:
  0.6 19.5 %shard_map.41 = (f32[1,1,64,8192]{3,2,1,0:T(8,128)S(1)}, f32[2,8,16,128]{3,2,1,0:T(8,128)S(1)}, bf16[384,512]{1,0:T(8,128)(2,1)S(1)}, bf16[64,48]{1,0:T(8,128)(2,1)S(1)}) custom-call(f32[1,1,64,8192]{3,2,1,0:T(8,128)} %x_hbm.1, f32[208,256]{1,0:T(8,128)} %constant.2.clone.table_hbm), custom_call_target="tpu_custom_call" | custom-call | tf_op jit(solution)/shard_map/pallas_call | solution.py:296
  20.2 1.7 %shard_map.42 = (f32[1,1,64,8192]{3,2,1,0:T(8,128)}, bf16[1,64,8192]{2,1,0:T(8,128)(2,1)}) custom-call(f32[1,1,64,8192]{3,2,1,0:T(8,128)S(1)} %get-tuple-element.6.fresh_in, f32[2,8,16,128]{3,2,1,0:T(8,128)S(1)} %get-tuple-element.7.later, bf16[384,512]{1,0:T(8,128)(2,1)S(1)} %get-tuple-element.8.dec_cols, bf16[64,48]{1,0:T(8,128)(2,1)S(1)} %get-tuple-element.9.dec_rows), custom_call_target="tpu_custom_call" | custom-call | tf_op jit(solution)/shard_map/pallas_call | solution.py:329
